TPU v7x, 256 devices: a whole 4x4x8 slice. The times are simulated.
256 devices in a mesh: row: 16 (over z_lo, x), col: 16 (over y, z_hi, core).
Axes of the slice: x: 4, y: 4, z: 8 (z_hi: 2, z_lo: 4; z = z_hi * 4 + z_lo), core: 2. Of those that a mesh axis runs over, the one named last changes fastest.
Arguments:
- tiles: bfloat16 [1024, 64, 128, 128], P('row', 'col'), may hold values from -0.0625 to 0.0625
- pattern: int32 [1024, 64], P('row', 'col'), may hold values from 0 to 31, as said below
- omega: bfloat16 [65536, 128], P(('row', 'col')), may hold values from -6 to 6
Outputs:
- basis: float32 [65536, 128], P(('row', 'col'))
Inputs may be any that keep to these rules, and one draw needn't show every extreme that they name: `pattern`: within each row block and index of col the 4 entries are distinct.
All inputs are finite; a program needn't handle non-finite values.
Results may differ from a plain program's by a relative error of at most 0.0065.
Values may be sent and summed in bfloat16 or wider, within the bound.
A program may use at most 128 MiB of HBM per device.

v0:
```python
import jax
import jax.numpy as jnp
from jax import lax
from jax.sharding import PartitionSpec as P


def local(tiles, pattern, omega):
    row_blocks, tile_count, bsize, unused = tiles.shape
    width = omega.shape[1]
    gathered = lax.all_gather(omega, "row", axis=0, tiled=True)
    groups = gathered.shape[0] // bsize
    blocks = gathered.reshape(groups, bsize, width)
    chosen = blocks[pattern]
    partial_value = jnp.einsum("itab,itbk->iak", tiles, chosen, preferred_element_type=jnp.float32)
    partial_value = partial_value.reshape(row_blocks * bsize, width)
    probe = lax.psum(partial_value, "col").astype(jnp.bfloat16)
    probe = probe.reshape(row_blocks, bsize, width)
    terms = jnp.einsum("itab,iak->itbk", tiles, probe, preferred_element_type=jnp.float32)
    terms = terms.reshape(row_blocks * tile_count, bsize * width)
    onehot = (pattern.reshape(-1)[:, None] == jnp.arange(groups, dtype=jnp.int32)[None, :]).astype(
        jnp.float32
    )
    sketch_part = jnp.dot(onehot.T, terms, precision=lax.Precision.HIGH).reshape(
        groups * bsize, width
    )
    total_cols = groups * bsize * lax.axis_size("col")
    sketch = lax.psum_scatter(sketch_part, "row", scatter_dimension=0, tiled=True)
    gram = lax.psum(jnp.dot(sketch.T, sketch, precision=lax.Precision.HIGHEST), ("row", "col"))
    lower = jnp.linalg.cholesky(gram)
    solved = jax.scipy.linalg.solve_triangular(lower, sketch.T, lower=True)
    return solved.T * jnp.sqrt(jnp.float32(total_cols))


def solution(mesh):
    return jax.shard_map(
        local,
        mesh=mesh,
        in_specs=(P("row", "col", None, None), P("row", "col"), P(("row", "col"), None)),
        out_specs=P(("row", "col"), None),
        check_vma=False,
    )
```

profile of v0, /device:TPU:1, one launch (start us, length us, event | category | flops | bytes accessed | tf_op | source)
XLA Modules:
  0.0 702.7 jit_solution(1653958004985712216)
XLA Ops:
  6.5 0.0 all-gather.2.cloned.1.call-start
  6.5 0.7 all-gather.2.cloned.1.call-update
  7.3 0.0 reduce-scatter.2.cloned.1.call-start
  7.3 0.8 copy.6
  8.1 0.7 compare_select_fusion
  8.8 0.1 copy.7
  8.9 0.1 reshape.33
  9.0 0.1 eq.15
  9.1 74.6 %all-gather.2.cloned.1.call-done = bf16[4096,128]{1,0:T(8,128)(2,1)} async-done(((bf16[256,128]{1,0:T(8,128)(2,1)}), bf16[4096,128]{1,0:T(8,128)(2,1)}) %all-gather.2.cloned.1.call-update) | async-done | bytes 1048592 | tf_op jit(solution)/shard_map/all_gather | solution.py:10
  83.7 9.8 %gather_fusion = bf16[256,128,128]{2,1,0:T(8,128)(2,1)} fusion(bf16[32,128,128]{2,1,0:T(8,128)(2,1)} %bitcast.37, s32[1024]{0:T(1024)S(1)} %pad_clamp_fusion), kind=kCustom, calls=%fused_computation | custom fusion | bytes 16778240 | tf_op jit(solution)/shard_map/gather | solution.py:13
  93.5 10.1 %fusion.8 = f32[64,128,128,1]{1,2,3,0:T(8,128)} fusion(bf16[64,4,128,128]{3,2,1,0:T(8,128)(2,1)} %param.3, bf16[64,4,128,128]{3,2,1,0:T(8,128)(2,1)} %bitcast.38), kind=kOutput, calls=%fused_computation.20 | convolution fusion | flops 1073741824 | bytes 20971520 | tf_op jit(solution)/shard_map/itab,itbk->iak/dot_general | solution.py:14
  103.6 190.4 %all-reduce.4 = bf16[8192,128]{1,0:T(8,128)(2,1)S(1)} all-reduce(f32[8192,128]{1,0:T(8,128)} %bitcast.39), channel_id=1, replica_groups=mesh['row'=16,'col'=16] {'col'}, use_global_device_ids=true, to_apply=%region_0.0 | all-reduce | flops 1048576 | bytes 6291456 | tf_op jit(solution)/shard_map/psum | solution.py:16
  294.0 11.5 %convolution_bitcast_fusion = f32[64,4,128,128]{2,3,1,0:T(8,128)} fusion(bf16[64,128,128,1]{2,1,3,0:T(8,128)(2,1)S(1)} %bitcast.40, bf16[64,4,128,128]{3,2,1,0:T(8,128)(2,1)} %param.3), kind=kOutput, calls=%fused_computation.4 | convolution fusion | flops 1073741824 | bytes 27262976 | tf_op jit(solution)/shard_map/itab,iak->itbk/dot_general | solution.py:18
  305.5 17.5 %copy.9 = f32[64,4,128,128]{3,2,1,0:T(8,128)} copy(f32[64,4,128,128]{2,3,1,0:T(8,128)} %convolution_bitcast_fusion) | data formatting | bytes 33554432 | tf_op jit(solution)/shard_map/itab,iak->itbk/dot_general | solution.py:18
  322.9 17.2 %fusion = f32[32,16384]{1,0:T(8,128)S(1)} fusion(f32[32,8,128,128]{3,2,1,0:T(8,128)} %bitcast.36, s32[256]{0:T(256)S(1)} %eq.15), kind=kOutput, calls=%fused_computation.1 | convolution fusion | flops 805314560 | bytes 18875392 | tf_op jit(solution)/shard_map/dot_general | solution.py:23
  340.1 1.5 reshape.30
  341.6 0.0 reduce-scatter.2.cloned.1.call-update
  341.7 0.3 all-reduce.3.cloned.1.call-start
  341.9 77.9 %reduce-scatter.2.cloned.1.call-done = f32[256,128]{1,0:T(8,128)} async-done(((f32[4096,128]{1,0:T(8,128)}), f32[256,128]{1,0:T(8,128)}) %reduce-scatter.2.cloned.1.call-update) | async-done | bytes 131088 | tf_op jit(solution)/shard_map/reduce_scatter | solution.py:27
  419.8 2.0 fusion.7
  421.8 0.0 all-reduce.3.cloned.1.call-update
  421.8 247.8 %all-reduce.3.cloned.1.call-done = f32[128,128]{0,1:T(8,128)} async-done(((f32[128,128]{0,1:T(8,128)}), f32[128,128]{0,1:T(8,128)}) %all-reduce.3.cloned.1.call-update) | async-done | bytes 65552 | tf_op jit(solution)/shard_map/psum | solution.py:28
  669.6 0.9 copy.11
  670.6 0.9 fusion.5
  671.4 11.7 %cholesky.16 = f32[128,128]{1,0:T(8,128)S(1)} custom-call(f32[128,128]{1,0:T(8,128)S(1)} %fusion.5), custom_call_target="Cholesky" | custom-call | tf_op jit(solution)/shard_map/jit(cholesky)/cholesky | solution.py:29
  683.2 0.6 compare_reduce_fusion
  683.8 0.7 fusion.3
  684.5 9.8 %custom-call.7 = f32[1,128,128]{1,2,0:T(8,128)S(1)} custom-call(f32[1,128,128]{2,1,0:T(8,128)S(1)} %fusion.3), custom_call_target="InvertDiagBlocksLowerTriangular" | custom-call | tf_op jit(solution)/shard_map/jit(_solve_triangular)/triangular_solve | solution.py:30
  694.3 1.8 convolution_multiply_fusion
  (2 shorter events, 0.0 us)
Async XLA Ops:
  6.5 77.2 %all-gather.2.cloned.1.call-start = ((), (), s32[]{:S(2)}) async-start(), calls=%async_computation.1 | async-start | bytes 1114112 | tf_op jit(solution)/shard_map/all_gather | solution.py:10
  7.3 412.6 %reduce-scatter.2.cloned.1.call-start = ((), (), s32[]{:S(2)}) async-start(), calls=%async_computation.2 | async-start | bytes 2228224 | tf_op jit(solution)/shard_map/reduce_scatter | solution.py:27
  341.7 328.0 %all-reduce.3.cloned.1.call-start = ((), (), s32[]{:S(2)}) async-start(), calls=%async_computation.3 | async-start | bytes 131072 | tf_op jit(solution)/shard_map/psum | solution.py:28
Sparse Core Ops, SparseCore 0:
  9.1 74.5 all-gather.1
  341.8 77.9 reduce-scatter.1
  425.3 244.2 all-reduce.2
where the time goes:
time: 703 us
  waiting for transfers between devices  401 us (57%)
  blocking collectives  190 us (27%)
  matrix products  42.6 us (6%)
  local copies, waits for them, and re-layouts  30.8 us (4%)
  other arithmetic  24.4 us (3%)
  between operations  13.2 us (2%)
    psum x1, waiting for transfers between devices, local(): lax.psum(jnp.dot(sketch.T, sketch, precision=lax.Precision.HIGHEST), ('ro...  248 us
    psum x1, blocking collectives, local(): probe = lax.psum(partial_value, 'col').astype(jnp.bfloat16)  190 us
    reduce_scatter x1, waiting for transfers between devices, local(): lax.psum_scatter(sketch_part, 'row', scatter_dimension=0, tiled=True)  77.9 us
    all_gather x1, waiting for transfers between devices, local(): gathered = lax.all_gather(omega, 'row', axis=0, tiled=True)  74.6 us
    dot_general x1, local copies, waits for them, and re-layouts, local(): jnp.einsum('itab,iak->itbk', tiles, probe, preferred_element_type=jnp.flo...  17.5 us
    dot_general x1, matrix products, local(): jnp.dot(onehot.T, terms, precision=lax.Precision.HIGH)  17.2 us
  transfers between devices with their start and end apart: 3, of which 3 were waited for; matrix products, arithmetic and copies ran while one was open for 0% of the time, Pallas kernels for 0%

commit v1 on v0

v1 whole, which is shorter than its diff:
```python
import functools

import jax
import jax.numpy as jnp
from jax import lax
from jax.experimental import pallas as pl
from jax.experimental.pallas import tpu as pltpu
from jax.sharding import PartitionSpec as P

MESH = pl.DeviceIdType.MESH
BS = 128
F32 = jnp.float32
BF16 = jnp.bfloat16

OM_Z, OM_X, CORE_R, Y_R, Z_R, Y_G, CORE_G, SK_X, SK_Z, GR_P, GR_Z, GR_G = (
    0, 3, 15, 19, 31, 35, 47, 51, 63, 66, 98, 106)
N_SEM = 138


def outer_step(a, limit):
    rows = lax.broadcasted_iota(jnp.int32, (BS, BS), 0)
    cols = lax.broadcasted_iota(jnp.int32, (BS, BS), 1)
    done = []
    for k in range(8):
        row = a[k:k + 1, :]
        pivot = row[:, k:k + 1]
        col = jnp.broadcast_to(a[:, k:k + 1], (BS, BS))
        inv = 1.0 / pivot
        live = (rows > k) & (rows < limit)
        f = jnp.where(live, col * inv, 0.0)
        one = jnp.where(cols[:1] == k, 1.0, row)
        a = jnp.where(live & (cols == k), 0.0, a) - f * one
        done.append(pivot)
    return a, done


def lower_inverse(gram_ref, work_ref, piv_ref):
    work_ref[...] = gram_ref[...]

    def panel(p, carry):
        a, done = outer_step(work_ref[...], BS - 8 * p)
        piv_ref[pl.ds(pl.multiple_of(8 * p, 8), 8), :] = jnp.broadcast_to(
            jnp.concatenate(done, axis=0), (8, BS))
        a = jnp.concatenate([a[8:], a[:8]], axis=0)
        work_ref[...] = jnp.concatenate([a[:, 8:], a[:, :8]], axis=1)
        return carry

    lax.fori_loop(0, BS // 8, panel, 0)
    rows = lax.broadcasted_iota(jnp.int32, (BS, BS), 0)
    cols = lax.broadcasted_iota(jnp.int32, (BS, BS), 1)
    unit = jnp.where(rows > cols, work_ref[...], jnp.where(rows == cols, 1.0, 0.0))
    work_ref[...] = unit * lax.rsqrt(piv_ref[...])


def kernel(scale, pat, order, tiles_hbm, omega_hbm, out_ref,
           tiles, om, csend, crecv, own, ysend, yown, yrecv, zsend, zown, zrecv, probe_t, prefix, sk, skown,
           xrecv, zsum, zpiece, skrecv, skt, gpart, gown, grecv, gsum, gzrecv, gram, work, piv, ssem, rsem, lsem):
    r = lax.axis_index("row")
    c = lax.axis_index("col")
    zl, x = r // 4, r % 4
    y, zh, k = c // 4, (c // 2) % 2, c % 2

    def dev(zl=zl, x=x, y=y, zh=zh, k=k):
        return (zl * 4 + x, y * 4 + zh * 2 + k)

    def plane(d):
        n = ((x * 4 + y) * 2 + k + d) % 32
        return dev(x=n // 8, y=(n // 2) % 4, k=n % 2)

    def along_z(d):
        n = (zh * 4 + zl + d) % 8
        return dev(zh=n // 4, zl=n % 4)

    def send(src, dst, sem, where):
        pltpu.make_async_remote_copy(src_ref=src, dst_ref=dst, send_sem=ssem.at[sem], recv_sem=rsem.at[sem],
                                     device_id=where, device_id_type=MESH).start()

    def got(ref, sem):
        pltpu.make_async_copy(ref, ref, rsem.at[sem]).wait()

    def sent(ref, sem):
        pltpu.make_async_copy(ref, ref, ssem.at[sem]).wait()

    load_tiles = pltpu.make_async_copy(tiles_hbm, tiles, lsem.at[0])
    load_tiles.start()
    mine = om.at[pl.ds(2 * r, 2)]
    load_omega = pltpu.make_async_copy(omega_hbm, mine, lsem.at[1])
    load_omega.start()

    with jax.named_scope("barrier"):
        barrier = pltpu.get_barrier_semaphore()

        def greet_plane(d, carry):
            pl.semaphore_signal(barrier, inc=1, device_id=plane(d), device_id_type=MESH)
            return carry

        def greet_z(d, carry):
            pl.semaphore_signal(barrier, inc=1, device_id=along_z(d), device_id_type=MESH)
            return carry

        lax.fori_loop(1, 32, greet_plane, 0)
        lax.fori_loop(1, 8, greet_z, 0)
        load_omega.wait()
        pl.semaphore_wait(barrier, 38)

    with jax.named_scope("omega_gather"):
        for d in (3, 2, 1):
            send(mine, mine, OM_Z + d - 1, dev(zl=(zl + d) % 4))
        for dx in (1, 2, 3):
            send(mine, mine, OM_X + dx - 1, dev(x=(x + dx) % 4))
        for d in (1, 2, 3):
            block = om.at[pl.ds(2 * (((zl + 4 - d) % 4) * 4 + x), 2)]
            got(block, OM_Z + d - 1)
            for dx in (1, 2, 3):
                send(block, block, OM_X + d * 3 + dx - 1, dev(x=(x + dx) % 4))
        load_tiles.wait()
        for d in range(4):
            for dx in (1, 2, 3):
                got(om.at[pl.ds(2 * (((zl + 4 - d) % 4) * 4 + (x + 4 - dx) % 4), 2)], OM_X + d * 3 + dx - 1)
        for d in (1, 2, 3):
            sent(mine, OM_Z + d - 1)
        for d in range(4):
            for dx in (1, 2, 3):
                sent(mine, OM_X + d * 3 + dx - 1)

    def product(i):
        left = jnp.concatenate([tiles[i, t] for t in range(4)], axis=1)
        right = jnp.concatenate([om[pat[i, t]] for t in range(4)], axis=0)
        return jnp.dot(left, right, preferred_element_type=F32)

    def value_part(m):
        def for_sibling(b, carry):
            csend[m, b] = product(((1 - k) * 4 + m) * 8 + b).astype(BF16)
            return carry

        def for_own(b, carry):
            own[m, b] = product((k * 4 + m) * 8 + b)
            return carry

        lax.fori_loop(0, 8, for_sibling, 0, unroll=True)
        send(csend.at[m], crecv.at[m], CORE_R + m, dev(k=1 - k))
        lax.fori_loop(0, 8, for_own, 0, unroll=True)

    def along_y(m):
        got(crecv.at[m], CORE_R + m)
        for d in (1, 2, 3, 0):
            b = ((y + d) % 4) * 2
            total = own[m, pl.ds(b, 2)] + crecv[m, pl.ds(b, 2)].astype(F32)
            if d:
                ysend[m, d - 1] = total.astype(BF16)
                send(ysend.at[m, d - 1], yrecv.at[m, d - 1], Y_R + m * 3 + d - 1, dev(y=(y + d) % 4))
            else:
                yown[m] = total

    def across_z(m):
        total = yown[m]
        for d in (1, 2, 3):
            got(yrecv.at[m, d - 1], Y_R + m * 3 + d - 1)
            total += yrecv[m, d - 1].astype(F32)
        zown[m] = total
        zsend[m] = total.astype(BF16)
        send(zsend.at[m], zrecv.at[m], Z_R + m, dev(zh=1 - zh))

    def gather_y(m):
        got(zrecv.at[m], Z_R + m)
        total = zown[m] + zrecv[m].astype(F32)
        at = (k * 4 + m) * 8 + y * 2
        for b in range(2):
            probe_t[at + b] = total[b].T.astype(BF16)
        part = probe_t.at[pl.ds(at, 2)]
        for d in (1, 2, 3):
            send(part, part, Y_G + m * 3 + d - 1, dev(y=(y + d) % 4))

    def gather_core(m):
        for d in (1, 2, 3):
            got(probe_t.at[pl.ds((k * 4 + m) * 8 + ((y + 4 - d) % 4) * 2, 2)], Y_G + m * 3 + d - 1)
        part = probe_t.at[pl.ds((k * 4 + m) * 8, 8)]
        send(part, part, CORE_G + m, dev(k=1 - k))

    with jax.named_scope("probe_value"):
        value_part(0)
        value_part(1)
        along_y(0)
        value_part(2)
        along_y(1)
        value_part(3)
        along_y(2)
        along_y(3)
    with jax.named_scope("probe_sum"):
        across_z(0)
        across_z(1)
        across_z(2)
        gather_y(0)
        across_z(3)
        gather_y(1)
        gather_y(2)
        gather_core(0)
        gather_y(3)
        gather_core(1)
        gather_core(2)
        gather_core(3)
        for m in range(4):
            got(probe_t.at[pl.ds(((1 - k) * 4 + m) * 8, 8)], CORE_G + m)
        for m in range(4):
            sent(csend.at[m], CORE_R + m)
            sent(zsend.at[m], Z_R + m)
            sent(crecv.at[m], CORE_G + m)
            for d in range(3):
                sent(ysend.at[m, d], Y_R + m * 3 + d)
                sent(ysend.at[m, d], Y_G + m * 3 + d)

    with jax.named_scope("sketch_value"):
        def term(s, acc):
            e = order[s]
            keep = order[256 + s].astype(F32)
            acc = acc * keep + jnp.dot(probe_t[e // 4], tiles[e // 4, e % 4], preferred_element_type=F32)
            prefix[s] = acc
            return acc

        lax.fori_loop(0, 256, term, jnp.zeros((BS, BS), F32), unroll=8)

    with jax.named_scope("sketch_sum"):
        def column(p):
            return prefix[order[512 + p]] * order[544 + p].astype(F32)

        for dz in (1, 2, 3, 0):
            for dx in (1, 2, 3):
                to = ((zl + dz) % 4) * 4 + (x + dx) % 4
                for b in range(2):
                    sk[dz, dx - 1, b] = column(2 * to + b).astype(BF16)
                send(sk.at[dz, dx - 1], xrecv.at[dz, dx - 1], SK_X + dz * 3 + dx - 1, dev(x=(x + dx) % 4))
        for dz in (1, 2, 3, 0):
            for b in range(2):
                skown[dz, b] = column(2 * (((zl + dz) % 4) * 4 + x) + b)
        for dz in (1, 2, 3, 0):
            total = skown[dz]
            for dx in (1, 2, 3):
                got(xrecv.at[dz, dx - 1], SK_X + dz * 3 + dx - 1)
                total += xrecv[dz, dx - 1].astype(F32)
            if dz:
                zpiece[dz - 1] = total.astype(BF16)
                send(zpiece.at[dz - 1], skrecv.at[dz - 1], SK_Z + dz - 1, dev(zl=(zl + dz) % 4))
            else:
                zsum[...] = total
        total = zsum[...]
        for dz in (1, 2, 3):
            got(skrecv.at[dz - 1], SK_Z + dz - 1)
            total += skrecv[dz - 1].astype(F32)
        skt[:, :BS] = total[0]
        skt[:, BS:] = total[1]
        for dz in range(4):
            for dx in range(3):
                sent(sk.at[dz, dx], SK_X + dz * 3 + dx)
        for dz in range(3):
            sent(zpiece.at[dz], SK_Z + dz)

    with jax.named_scope("gram_sum"):
        g = lax.dot_general(skt[...], skt[...], (((1,), (1,)), ((), ())), precision=lax.Precision.HIGHEST,
                            preferred_element_type=F32)
        for n in range(32):
            gpart[n] = g[4 * n:4 * n + 4]
        here = (x * 4 + y) * 2 + k

        def spread(d, carry):
            send(gpart.at[(here + d) % 32], grecv.at[d - 1], GR_P + d, plane(d))
            return carry

        lax.fori_loop(1, 32, spread, 0)

        def collect(d, carry):
            got(grecv.at[d - 1], GR_P + d)
            return carry

        lax.fori_loop(1, 32, collect, 0)
        gsum[...] = gpart[here] + jnp.sum(grecv[...], axis=0)
        for d in range(1, 8):
            send(gsum, gzrecv.at[d - 1], GR_Z + d, along_z(d))
        for d in range(1, 8):
            got(gzrecv.at[d - 1], GR_Z + d)
        gown[here] = gsum[...] + jnp.sum(gzrecv[...], axis=0)

        def share(d, carry):
            send(gown.at[here], gown.at[here], GR_G + d, plane(d))
            return carry

        lax.fori_loop(1, 32, share, 0)

        def receive(d, carry):
            got(gown.at[(here + 32 - d) % 32], GR_G + d)
            return carry

        lax.fori_loop(1, 32, receive, 0)
        for n in range(32):
            gram[4 * n:4 * n + 4, :] = gown[n]

        def drain(d, carry):
            sent(gsum, GR_P + d)
            sent(gsum, GR_G + d)
            return carry

        lax.fori_loop(1, 32, drain, 0)
        for d in range(1, 8):
            sent(gsum, GR_Z + d)

    with jax.named_scope("cholesky"):
        lower_inverse(gram, work, piv)
    with jax.named_scope("basis"):
        basis_t = jnp.dot(work[...], skt[...], precision=lax.Precision.HIGHEST, preferred_element_type=F32)
        out_ref[...] = basis_t.T * scale


def sorted_order(pattern, groups):
    flat = pattern.reshape(-1)
    count = flat.shape[0]
    place = jnp.arange(count, dtype=jnp.int32)
    key = flat * count + place
    rank = jnp.sum((key[None, :] < key[:, None]).astype(jnp.int32), axis=1)
    at = rank[None, :] == place[:, None]
    tile = jnp.sum(jnp.where(at, place[None, :], 0), axis=1)
    block = jnp.sum(jnp.where(at, flat[None, :], 0), axis=1)
    keep = jnp.concatenate([jnp.zeros(1, jnp.int32), (block[1:] == block[:-1]).astype(jnp.int32)])
    wanted = jnp.arange(groups, dtype=jnp.int32)
    last = jnp.maximum(jnp.sum((flat[None, :] <= wanted[:, None]).astype(jnp.int32), axis=1) - 1, 0)
    some = jnp.any(flat[None, :] == wanted[:, None], axis=1).astype(jnp.int32)
    return jnp.concatenate([tile, keep, last, some])


def local(tiles, pattern, omega):
    scale = float(256 * omega.shape[0]) ** 0.5
    order = sorted_order(pattern, 32)
    vmem = pltpu.VMEM
    return pl.pallas_call(
        functools.partial(kernel, scale),
        name="gauss_newton_sketch",
        out_shape=jax.ShapeDtypeStruct((2 * BS, BS), F32),
        in_specs=[pl.BlockSpec(memory_space=pltpu.SMEM)] * 2 + [pl.BlockSpec(memory_space=pl.ANY)] * 2,
        out_specs=pl.BlockSpec(memory_space=vmem),
        scratch_shapes=[
            vmem((64, 4, BS, BS), BF16),
            vmem((32, BS, BS), BF16),
            vmem((4, 8, BS, BS), BF16),
            vmem((4, 8, BS, BS), BF16),
            vmem((4, 8, BS, BS), F32),
            vmem((4, 3, 2, BS, BS), BF16),
            vmem((4, 2, BS, BS), F32),
            vmem((4, 3, 2, BS, BS), BF16),
            vmem((4, 2, BS, BS), BF16),
            vmem((4, 2, BS, BS), F32),
            vmem((4, 2, BS, BS), BF16),
            vmem((64, BS, BS), BF16),
            vmem((256, BS, BS), F32),
            vmem((4, 3, 2, BS, BS), BF16),
            vmem((4, 2, BS, BS), F32),
            vmem((4, 3, 2, BS, BS), BF16),
            vmem((2, BS, BS), F32),
            vmem((3, 2, BS, BS), BF16),
            vmem((3, 2, BS, BS), BF16),
            vmem((BS, 2 * BS), F32),
            vmem((32, 4, BS), F32),
            vmem((32, 4, BS), F32),
            vmem((31, 4, BS), F32),
            vmem((4, BS), F32),
            vmem((7, 4, BS), F32),
            vmem((BS, BS), F32),
            vmem((BS, BS), F32),
            vmem((BS, BS), F32),
            pltpu.SemaphoreType.DMA((N_SEM,)),
            pltpu.SemaphoreType.DMA((N_SEM,)),
            pltpu.SemaphoreType.DMA((2,)),
        ],
        compiler_params=pltpu.CompilerParams(
            collective_id=0, has_side_effects=True, vmem_limit_bytes=56 * 1024 * 1024),
        cost_estimate=pl.CostEstimate(flops=2 * 2 * 256 * BS ** 3, bytes_accessed=9 * 2 ** 20, transcendentals=0),
    )(pattern, order, tiles, omega.reshape(2, BS, BS))


def solution(mesh):
    return jax.shard_map(
        local,
        mesh=mesh,
        in_specs=(P("row", "col", None, None), P("row", "col"), P(("row", "col"), None)),
        out_specs=P(("row", "col"), None),
        check_vma=False,
    )
```

time: 703 us -> 122 us (0.17)
  waiting for transfers between devices: 401 us -> 0 us
  blocking collectives: 190 us -> 0 us
  Pallas kernels: 0 us -> 118 us
  matrix products: 42.6 us -> 0 us
  local copies, waits for them, and re-layouts: 30.8 us -> 3.11 us
  other arithmetic: 24.4 us -> 0.66 us
  between operations: 13.2 us -> 0.04 us
    psum x1 -> x0, waiting for transfers between devices: 248 us -> none  [local(): lax.psum(jnp.dot(sketch.T, sketch, precision=lax.Precision.HIGHEST), ('ro...]
    psum x1 -> x0, blocking collectives: 190 us -> none  [local(): probe = lax.psum(partial_value, 'col').astype(jnp.bfloat16)]
    pallas_call x0 -> x1, Pallas kernels: none -> 118 us  [local(): pl.pallas_call(functools.partial(kernel, scale), name='gauss_newton_sketc...]
    reduce_scatter x1 -> x0, waiting for transfers between devices: 77.9 us -> none  [local(): lax.psum_scatter(sketch_part, 'row', scatter_dimension=0, tiled=True)]
    all_gather x1 -> x0, waiting for transfers between devices: 74.6 us -> none  [local(): gathered = lax.all_gather(omega, 'row', axis=0, tiled=True)]
    dot_general x4 -> x0, matrix products: 40.7 us -> none  [the longest x1 17.2 us: local(): jnp.dot(onehot.T, terms, precision=lax.Precision.HIGH)]
    another operation x5 -> x0, other arithmetic: 22.9 us -> none  [the longest x3 12.4 us: local(): lower = jnp.linalg.cholesky(gram)]
    dot_general x1 -> x0, local copies, waits for them, and re-layouts: 17.5 us -> none  [local(): jnp.einsum('itab,iak->itbk', tiles, probe, preferred_element_type=jnp.flo...]
  transfers between devices with their start and end apart: 3 -> 0, of which waited for: 3 -> 0; matrix products, arithmetic and copies ran while one was open for 0% -> 0% of each run, Pallas kernels for 0% -> 0%
where the time goes in v1:
time: 122 us; the launch traced here: 121 us
  Pallas kernels  118 us (97%)
  local copies, waits for them, and re-layouts  3.11 us (3%)
    pallas_call x1, Pallas kernels, local(): pl.pallas_call(functools.partial(kernel, scale), name='gauss_newton_sketc...  118 us

profile of v1, /device:TPU:1, one launch (start us, length us, event | category | flops | bytes accessed | tf_op | source)
XLA Modules:
  0.0 121.4 jit_solution(464161947679170334)
XLA Ops:
  0.0 0.8 copy.8.pat
  0.8 0.0 copy-start
  0.8 0.1 reshape.26
  0.9 0.1 fusion
  1.0 0.1 convert_reduce_fusion.1
  1.1 0.2 convert_reduce_fusion
  1.3 0.2 select_reduce_fusion
  1.5 0.1 compare_convert_fusion
  1.6 0.7 concatenate.3.order
  2.2 0.0 copy-done
  2.2 117.6 %gauss_newton_sketch.1 = f32[256,128]{1,0:T(8,128)} custom-call(s32[64,4]{1,0:T(8,128)} %copy-done, s32[576]{0:T(1024)} %concatenate.3.order, bf16[64,4,128,128]{3,2,1,0:T(8,128)(2,1)} %tiles_hbm.1, bf16[2,128,128]{2,1,0:T(8,128)(2,1)} %bitcast.1), custom_call_target="tpu_custom_call" | custom-call | flops 2147483648 | bytes 9437184 | tf_op jit(solution)/shard_map/gauss_newton_sketch/pallas_call | solution.py:332
  119.9 1.6 %copy.10 = f32[256,128]{1,0:T(8,128)} copy(f32[256,128]{1,0:T(8,128)} %gauss_newton_sketch.1) | data formatting | bytes 262144
  (3 shorter events, 0.0 us)
Async XLA Ops:
  0.8 1.5 %copy-start = (s32[64,4]{1,0:T(8,128)}, s32[64,4]{1,0:T(8,128)S(1)}, u32[]{:S(2)}) copy-start(s32[64,4]{1,0:T(8,128)S(1)} %copy.8.pat) | copy-start | bytes 3076

commit v2 on v1

v2 whole, which is shorter than its diff:
```python
import functools

import jax
import jax.numpy as jnp
from jax import lax
from jax.experimental import pallas as pl
from jax.experimental.pallas import tpu as pltpu
from jax.sharding import PartitionSpec as P

MESH = pl.DeviceIdType.MESH
BS = 128
F32 = jnp.float32
BF16 = jnp.bfloat16

OM_Z, OM_X, CORE_R, Y_R, Z_R, Y_G, CORE_G, SK_X, SK_Z, GR_P, GR_Z, GR_G = (
    0, 3, 15, 19, 31, 35, 47, 51, 63, 66, 82, 98)
N_SEM = 114
PAIRS = 144


def over_lanes(v, k):
    return jnp.broadcast_to(v[:, k:k + 1], (8, BS))


def over_rows(v, k):
    return jnp.broadcast_to(v[k:k + 1, :], (8, BS))


def lower_inverse(gram, out):
    rows = lax.broadcasted_iota(jnp.int32, (8, BS), 0)
    cols = lax.broadcasted_iota(jnp.int32, (8, BS), 1)
    on = [cols == rows + 8 * p for p in range(16)]
    diag = [jnp.where(on[p], gram[p], 0.0) for p in range(16)]
    across = lax.rsqrt(jnp.sum(functools.reduce(jnp.add, diag), axis=0, keepdims=True))
    a = [gram[p] * lax.rsqrt(jnp.sum(diag[p], axis=1, keepdims=True)) * across for p in range(16)]
    for p in range(16):
        panel, first = a[p], 8 * p
        block = [over_lanes(panel, first + j) for j in range(8)]
        below = [[over_lanes(a[q], first + j) for j in range(8)] for q in range(p + 1, 16)]
        for j in range(0, 8, 2):
            k = first + j
            c0, c1 = block[j], block[j + 1]
            r0, r1 = over_rows(panel, j), over_rows(panel, j + 1)
            pa, pb, pc = over_rows(c0, j), over_rows(c0, j + 1), over_rows(c1, j + 1)
            det = pa * pc - pb * pb
            inv = 1.0 / det
            r0 = jnp.where(cols == k, 1.0, jnp.where(cols == k + 1, 0.0, r0))
            r1 = jnp.where(cols == k + 1, 1.0, jnp.where(cols == k, 0.0, r1))
            root = lax.rsqrt(pa)
            out[k:k + 1, :] = (jnp.where(cols <= k, r0, 0.0) * root * across)[0:1]
            low = r1 - (pb * (root * root)) * r0
            out[k + 1:k + 2, :] = (jnp.where(cols <= k + 1, low, 0.0) * (lax.rsqrt(det) * (pa * root)) * across)[0:1]
            f0 = jnp.where(rows == j, -1.0, jnp.where(rows == j + 1, 0.0, c0))
            f1 = jnp.where(rows == j + 1, -1.0, jnp.where(rows == j, 0.0, c1))
            g0, g1 = (f0 * pc - f1 * pb) * inv, (f1 * pa - f0 * pb) * inv
            pair = (rows == j) | (rows == j + 1)
            for i in range(j + 2, 8):
                block[i] = jnp.where(pair, 0.0, block[i]) - (
                    g0 * over_rows(block[i], j) + g1 * over_rows(block[i], j + 1))
            panel = jnp.where((cols == k) | (cols == k + 1) | pair, 0.0, panel) - (g0 * r0 + g1 * r1)
        inside = (cols >= first) & (cols < first + 8)
        r = [over_rows(panel, j) for j in range(8)]
        for q in range(p + 1, 16):
            b = below[q - p - 1]
            t = [b[j] * r[j] + b[j + 1] * r[j + 1] for j in range(0, 8, 2)]
            a[q] = jnp.where(inside, 0.0, a[q]) - ((t[0] + t[1]) + (t[2] + t[3]))


def sort_tiles(pat, meta):
    n, wanted = pat.shape[0], 3 * BS
    lane = lax.broadcasted_iota(jnp.int32, (n, BS), 1)
    pick = [pat[:, t:t + 1] for t in range(4)]
    hot = [jnp.where(jnp.broadcast_to(p, (n, BS)) == lane, 1, 0) for p in pick]
    total = (hot[0] + hot[1]) + (hot[2] + hot[3])
    upto = total
    for s in (1, 2, 4, 8, 16, 32):
        upto += jnp.concatenate([jnp.zeros((s, BS), jnp.int32), upto[:-s]], axis=0)
    before = upto - total
    count = upto[n - 1:]
    pairs = (count + 1) // 2
    ends = jnp.broadcast_to(pairs, (8, BS))
    for s in (1, 2, 4, 8, 16):
        ends += jnp.concatenate([jnp.zeros((8, s), jnp.int32), ends[:, :-s]], axis=1)
    base = ends[0:1] - pairs
    wide = lax.broadcasted_iota(jnp.int32, (n, wanted), 1)
    first = lax.broadcasted_iota(jnp.int32, (n, wanted), 0) * 4
    tile = jnp.zeros((1, wanted), jnp.int32)
    fresh = jnp.zeros((1, wanted), jnp.int32)
    flat = jnp.zeros((1, wanted), jnp.int32)
    for t in range(4):
        rank = jnp.sum(hot[t] * before, axis=1, keepdims=True)
        at = rank + 2 * jnp.sum(hot[t] * base, axis=1, keepdims=True)
        before = before + hot[t]
        tile += jnp.sum(jnp.where(at == wide, first + (t - 256), 0), axis=0, keepdims=True)
        fresh += jnp.sum(jnp.where((at == 2 * wide) & (rank == 0), 1, 0), axis=0, keepdims=True)
        flat += jnp.sum(jnp.where(first + t == wide, pick[t], 0), axis=0, keepdims=True)
    meta[...] = jnp.zeros_like(meta)
    meta[0:1, :] = jnp.clip(tile + 256, 0, 256)
    meta[1:2, :] = 1 - fresh
    meta[2:3, :BS] = jnp.clip(base + pairs - 1, 0, PAIRS - 1)
    meta[3:4, :BS] = jnp.minimum(count, 1)
    meta[4:5, :] = jnp.clip(flat, 0, 31)


def kernel(pat_hbm, tiles_hbm, omega_hbm, gown, skt,
           tiles, om, csend, crecv, own, ysend, yown, yrecv, zsend, zown, zrecv, probe_t, prefix, sk, skown,
           xrecv, zsum, zpiece, skrecv, gpart, grecv, gsum, gzrecv, pat, meta, order, ssem, rsem, lsem):
    r = lax.axis_index("row")
    c = lax.axis_index("col")
    zl, x = r // 4, r % 4
    y, zh, k = c // 4, (c // 2) % 2, c % 2

    def dev(zl=zl, x=x, y=y, zh=zh, k=k):
        return (zl * 4 + x, y * 4 + zh * 2 + k)

    xs = [(x + d) % 4 for d in range(4)]
    ys = [(y + d) % 4 for d in range(4)]
    zs = [(zh * 4 + zl + d) % 8 for d in range(8)]

    def plane(d):
        return dev(x=xs[d // 4], y=ys[d % 4])

    def column(d):
        return dev(zh=zs[d // 2] // 4, zl=zs[d // 2] % 4, k=(k + d) % 2)

    def send(src, dst, sem, where):
        pltpu.make_async_remote_copy(src_ref=src, dst_ref=dst, send_sem=ssem.at[sem], recv_sem=rsem.at[sem],
                                     device_id=where, device_id_type=MESH).start()

    def got(ref, sem):
        pltpu.make_async_copy(ref, ref, rsem.at[sem]).wait()

    def sent(ref, sem):
        pltpu.make_async_copy(ref, ref, ssem.at[sem]).wait()

    load_pattern = pltpu.make_async_copy(pat_hbm, pat, lsem.at[2])
    load_pattern.start()
    load_tiles = pltpu.make_async_copy(tiles_hbm, tiles.at[pl.ds(0, 64)], lsem.at[0])
    load_tiles.start()
    mine = om.at[pl.ds(2 * r, 2)]
    load_omega = pltpu.make_async_copy(omega_hbm, mine, lsem.at[1])
    load_omega.start()

    with jax.named_scope("barrier"):
        barrier = pltpu.get_barrier_semaphore()

        for d in range(1, 16):
            pl.semaphore_signal(barrier, inc=1, device_id=plane(d), device_id_type=MESH)
            pl.semaphore_signal(barrier, inc=1, device_id=column(d), device_id_type=MESH)
        load_omega.wait()
        pl.semaphore_wait(barrier, 30)

    load_order = pltpu.make_async_copy(meta, order, lsem.at[3])

    with jax.named_scope("omega_gather"):
        for d in (3, 2, 1):
            send(mine, mine, OM_Z + d - 1, dev(zl=(zl + d) % 4))
        for dx in (1, 2, 3):
            send(mine, mine, OM_X + dx - 1, dev(x=(x + dx) % 4))
        tiles[64, 0] = jnp.zeros((BS, BS), BF16)
        probe_t[64] = jnp.zeros((BS, BS), BF16)
        load_pattern.wait()
        sort_tiles(pat, meta)
        load_order.start()
        for d in (1, 2, 3):
            block = om.at[pl.ds(2 * (((zl + 4 - d) % 4) * 4 + x), 2)]
            got(block, OM_Z + d - 1)
            for dx in (1, 2, 3):
                send(block, block, OM_X + d * 3 + dx - 1, dev(x=(x + dx) % 4))
        load_tiles.wait()
        load_order.wait()
        for d in range(4):
            for dx in (1, 2, 3):
                got(om.at[pl.ds(2 * (((zl + 4 - d) % 4) * 4 + (x + 4 - dx) % 4), 2)], OM_X + d * 3 + dx - 1)
        for d in (1, 2, 3):
            sent(mine, OM_Z + d - 1)
        for d in range(4):
            for dx in (1, 2, 3):
                sent(mine, OM_X + d * 3 + dx - 1)

    def product(i):
        left = jnp.concatenate([tiles[i, t] for t in range(4)], axis=1)
        right = jnp.concatenate([om[order[4, 4 * i + t]] for t in range(4)], axis=0)
        return jnp.dot(left, right, preferred_element_type=F32)

    def value_part(m):
        def for_sibling(b, carry):
            csend[m, b] = product(((1 - k) * 4 + m) * 8 + b).astype(BF16)
            return carry

        def for_own(b, carry):
            own[m, b] = product((k * 4 + m) * 8 + b)
            return carry

        lax.fori_loop(0, 8, for_sibling, 0, unroll=True)
        send(csend.at[m], crecv.at[m], CORE_R + m, dev(k=1 - k))
        lax.fori_loop(0, 8, for_own, 0, unroll=True)

    def along_y(m):
        got(crecv.at[m], CORE_R + m)
        for d in (1, 2, 3, 0):
            b = ((y + d) % 4) * 2
            total = own[m, pl.ds(b, 2)] + crecv[m, pl.ds(b, 2)].astype(F32)
            if d:
                ysend[m, d - 1] = total.astype(BF16)
                send(ysend.at[m, d - 1], yrecv.at[m, d - 1], Y_R + m * 3 + d - 1, dev(y=(y + d) % 4))
            else:
                yown[m] = total

    def across_z(m):
        total = yown[m]
        for d in (1, 2, 3):
            got(yrecv.at[m, d - 1], Y_R + m * 3 + d - 1)
            total += yrecv[m, d - 1].astype(F32)
        zown[m] = total
        zsend[m] = total.astype(BF16)
        send(zsend.at[m], zrecv.at[m], Z_R + m, dev(zh=1 - zh))

    def gather_y(m):
        got(zrecv.at[m], Z_R + m)
        total = zown[m] + zrecv[m].astype(F32)
        at = (k * 4 + m) * 8 + y * 2
        for b in range(2):
            probe_t[at + b] = total[b].T.astype(BF16)
        part = probe_t.at[pl.ds(at, 2)]
        for d in (1, 2, 3):
            send(part, part, Y_G + m * 3 + d - 1, dev(y=(y + d) % 4))

    def gather_core(m):
        for d in (1, 2, 3):
            got(probe_t.at[pl.ds((k * 4 + m) * 8 + ((y + 4 - d) % 4) * 2, 2)], Y_G + m * 3 + d - 1)
        part = probe_t.at[pl.ds((k * 4 + m) * 8, 8)]
        send(part, part, CORE_G + m, dev(k=1 - k))

    with jax.named_scope("probe_sum"):
        value_part(0)
        along_y(0)
        value_part(1)
        along_y(1)
        value_part(2)
        along_y(2)
        across_z(0)
        value_part(3)
        along_y(3)
        across_z(1)
        across_z(2)
        gather_y(0)
        across_z(3)
        gather_y(1)
        gather_y(2)
        gather_core(0)
        gather_y(3)
        gather_core(1)
        gather_core(2)
        gather_core(3)
        for m in range(4):
            got(probe_t.at[pl.ds(((1 - k) * 4 + m) * 8, 8)], CORE_G + m)
        for m in range(4):
            sent(csend.at[m], CORE_R + m)
            sent(zsend.at[m], Z_R + m)
            sent(crecv.at[m], CORE_G + m)
            for d in range(3):
                sent(ysend.at[m, d], Y_R + m * 3 + d)
                sent(ysend.at[m, d], Y_G + m * 3 + d)

    with jax.named_scope("sketch_value"):
        def term(q, acc):
            e, f = order[0, 2 * q], order[0, 2 * q + 1]
            left = jnp.concatenate([probe_t[e // 4], probe_t[f // 4]], axis=1)
            right = jnp.concatenate([tiles[e // 4, e % 4], tiles[f // 4, f % 4]], axis=0)
            acc = acc * order[1, q].astype(F32) + jnp.dot(left, right, preferred_element_type=F32)
            prefix[q] = acc
            return acc

        lax.fori_loop(0, PAIRS, term, jnp.zeros((BS, BS), F32), unroll=8)

    with jax.named_scope("sketch_sum"):
        def block_sum(p):
            return prefix[order[2, p]] * order[3, p].astype(F32)

        for dz in (1, 2, 3, 0):
            for dx in (1, 2, 3):
                to = ((zl + dz) % 4) * 4 + (x + dx) % 4
                for b in range(2):
                    sk[dz, dx - 1, b] = block_sum(2 * to + b).astype(BF16)
                send(sk.at[dz, dx - 1], xrecv.at[dz, dx - 1], SK_X + dz * 3 + dx - 1, dev(x=(x + dx) % 4))
        for dz in (1, 2, 3, 0):
            for b in range(2):
                skown[dz, b] = block_sum(2 * (((zl + dz) % 4) * 4 + x) + b)
        for dz in (1, 2, 3, 0):
            total = skown[dz]
            for dx in (1, 2, 3):
                got(xrecv.at[dz, dx - 1], SK_X + dz * 3 + dx - 1)
                total += xrecv[dz, dx - 1].astype(F32)
            if dz:
                zpiece[dz - 1] = total.astype(BF16)
                send(zpiece.at[dz - 1], skrecv.at[dz - 1], SK_Z + dz - 1, dev(zl=(zl + dz) % 4))
            else:
                zsum[...] = total
        total = zsum[...]
        for dz in (1, 2, 3):
            got(skrecv.at[dz - 1], SK_Z + dz - 1)
            total += skrecv[dz - 1].astype(F32)
        skt[:, :BS] = total[0]
        skt[:, BS:] = total[1]
        for dz in range(4):
            for dx in range(3):
                sent(sk.at[dz, dx], SK_X + dz * 3 + dx)
        for dz in range(3):
            sent(zpiece.at[dz], SK_Z + dz)

    with jax.named_scope("gram_sum"):
        g = lax.dot_general(skt[...], skt[...], (((1,), (1,)), ((), ())), precision=lax.Precision.HIGHEST,
                            preferred_element_type=F32)
        gpart[...] = g.reshape(16, 8, BS)
        here = x * 4 + y

        def total(own, parts):
            parts = [own] + [parts[d] for d in range(15)]
            while len(parts) > 1:
                parts = [parts[i] + parts[i + 1] for i in range(0, len(parts), 2)]
            return parts[0]

        for d in range(1, 16):
            send(gpart.at[xs[d // 4] * 4 + ys[d % 4]], grecv.at[d - 1], GR_P + d, plane(d))
        for d in range(1, 16):
            got(grecv.at[d - 1], GR_P + d)
        gsum[...] = total(gpart[here], grecv)
        for d in range(1, 16):
            send(gsum, gzrecv.at[d - 1], GR_Z + d, column(d))
        for d in range(1, 16):
            got(gzrecv.at[d - 1], GR_Z + d)
        gown[here] = total(gsum[...], gzrecv)
        for d in range(1, 16):
            send(gown.at[here], gown.at[here], GR_G + d, plane(d))
        for d in range(1, 16):
            got(gown.at[xs[(4 - d // 4) % 4] * 4 + ys[(4 - d % 4) % 4]], GR_G + d)
        for d in range(1, 16):
            sent(gsum, GR_P + d)
            sent(gsum, GR_Z + d)
            sent(gsum, GR_G + d)


def finish(scale, gram, skt, out_ref, work):
    lower_inverse(gram, work)
    basis_t = jnp.dot(work[...], skt[...], precision=lax.Precision.HIGHEST, preferred_element_type=F32)
    out_ref[...] = basis_t.T * scale


def local(tiles, pattern, omega):
    scale = float(256 * omega.shape[0]) ** 0.5
    vmem = pltpu.VMEM
    gram, sketch_t = pl.pallas_call(
        kernel,
        name="gauss_newton_sketch",
        out_shape=[jax.ShapeDtypeStruct((16, 8, BS), F32), jax.ShapeDtypeStruct((BS, 2 * BS), F32)],
        in_specs=[pl.BlockSpec(memory_space=pl.ANY)] * 3,
        out_specs=[pl.BlockSpec(memory_space=vmem)] * 2,
        scratch_shapes=[
            vmem((65, 4, BS, BS), BF16),
            vmem((32, BS, BS), BF16),
            vmem((4, 8, BS, BS), BF16),
            vmem((4, 8, BS, BS), BF16),
            vmem((4, 8, BS, BS), F32),
            vmem((4, 3, 2, BS, BS), BF16),
            vmem((4, 2, BS, BS), F32),
            vmem((4, 3, 2, BS, BS), BF16),
            vmem((4, 2, BS, BS), BF16),
            vmem((4, 2, BS, BS), F32),
            vmem((4, 2, BS, BS), BF16),
            vmem((65, BS, BS), BF16),
            vmem((PAIRS, BS, BS), F32),
            vmem((4, 3, 2, BS, BS), BF16),
            vmem((4, 2, BS, BS), F32),
            vmem((4, 3, 2, BS, BS), BF16),
            vmem((2, BS, BS), F32),
            vmem((3, 2, BS, BS), BF16),
            vmem((3, 2, BS, BS), BF16),
            vmem((16, 8, BS), F32),
            vmem((15, 8, BS), F32),
            vmem((8, BS), F32),
            vmem((15, 8, BS), F32),
            vmem((64, 4), jnp.int32),
            vmem((8, 3 * BS), jnp.int32),
            pltpu.SMEM((8, 3 * BS), jnp.int32),
            pltpu.SemaphoreType.DMA((N_SEM,)),
            pltpu.SemaphoreType.DMA((N_SEM,)),
            pltpu.SemaphoreType.DMA((4,)),
        ],
        compiler_params=pltpu.CompilerParams(
            collective_id=0, has_side_effects=True, vmem_limit_bytes=56 * 1024 * 1024),
        cost_estimate=pl.CostEstimate(flops=2 * 2 * 256 * BS ** 3, bytes_accessed=9 * 2 ** 20, transcendentals=0),
    )(pattern, tiles, omega.reshape(2, BS, BS))
    return pl.pallas_call(
        functools.partial(finish, scale),
        name="cholesky_basis",
        out_shape=jax.ShapeDtypeStruct((2 * BS, BS), F32),
        in_specs=[pl.BlockSpec(memory_space=vmem)] * 2,
        out_specs=pl.BlockSpec(memory_space=vmem),
        scratch_shapes=[vmem((BS, BS), F32)],
    )(gram, sketch_t)


def solution(mesh):
    return jax.shard_map(
        local,
        mesh=mesh,
        in_specs=(P("row", "col", None, None), P("row", "col"), P(("row", "col"), None)),
        out_specs=P(("row", "col"), None),
        check_vma=False,
    )
```

time: 122 us -> 103 us (0.84)
  Pallas kernels: 118 us -> 101 us
  local copies, waits for them, and re-layouts: 3.11 us -> 1.38 us
    pallas_call x1 -> x2, Pallas kernels: 118 us -> 101 us  [the longest x1 95.1 us: local(): pl.pallas_call(kernel, name='gauss_newton_sketch', out_shape=[jax.ShapeDt...]
where the time goes in v2:
time: 103 us
  Pallas kernels  101 us (98%)
  local copies, waits for them, and re-layouts  1.38 us (1%)
    pallas_call x1, Pallas kernels, local(): pl.pallas_call(kernel, name='gauss_newton_sketch', out_shape=[jax.ShapeDt...  95.1 us
    pallas_call x1, Pallas kernels, local(): pl.pallas_call(functools.partial(finish, scale), name='cholesky_basis', o...  6.35 us

profile of v2, /device:TPU:1, one launch (start us, length us, event | category | flops | bytes accessed | tf_op | source)
XLA Modules:
  0.0 102.8 jit_solution(6025032484813052279)
XLA Ops:
  0.0 1.4 %copy.4.pat_hbm = s32[64,4]{1,0:T(8,128)} copy(s32[64,4]{0,1:T(4,128)} %param.4) | data formatting | bytes 2048 | tf_op args[1]
  1.4 95.1 %gauss_newton_sketch.1 = (f32[16,8,128]{2,1,0:T(8,128)}, f32[128,256]{1,0:T(8,128)}) custom-call(s32[64,4]{1,0:T(8,128)} %copy.4.pat_hbm, bf16[64,4,128,128]{3,2,1,0:T(8,128)(2,1)} %tiles_hbm.1, bf16[2,128,128]{2,1,0:T(8,128)(2,1)} %bitcast.1), custom_call_target="tpu_custom_call" | custom-call | flops 2147483648 | bytes 9437184 | tf_op jit(solution)/shard_map/gauss_newton_sketch/pallas_call | solution.py:353
  96.5 6.3 %cholesky_basis.1 = f32[256,128]{1,0:T(8,128)} custom-call(f32[16,8,128]{2,1,0:T(8,128)} %get-tuple-element.7.gram, f32[128,256]{1,0:T(8,128)} %get-tuple-element.8.skt), custom_call_target="tpu_custom_call" | custom-call | tf_op jit(solution)/shard_map/cholesky_basis/pallas_call | solution.py:394

commit v3 on v2

--- a/solution.py
+++ b/solution.py
@@ -13,8 +13,8 @@
 BF16 = jnp.bfloat16
 
 OM_Z, OM_X, CORE_R, Y_R, Z_R, Y_G, CORE_G, SK_X, SK_Z, GR_P, GR_Z, GR_G = (
-    0, 3, 15, 19, 31, 35, 47, 51, 63, 66, 82, 98)
-N_SEM = 114
+    0, 3, 19, 23, 47, 51, 67, 71, 95, 98, 114, 130)
+N_SEM = 146
 PAIRS = 144
 
 
@@ -67,9 +67,11 @@
 
 
 def sort_tiles(pat, meta):
-    n, wanted = pat.shape[0], 3 * BS
+    n, wanted = pat.shape[1], 3 * BS
     lane = lax.broadcasted_iota(jnp.int32, (n, BS), 1)
-    pick = [pat[:, t:t + 1] for t in range(4)]
+    wide_pat = jnp.concatenate([pat[...], jnp.zeros((4, BS - n), jnp.int32)], axis=1)
+    tall = jnp.concatenate([wide_pat, jnp.zeros((4, BS), jnp.int32)], axis=0).T
+    pick = [tall[:n, t:t + 1] for t in range(4)]
     hot = [jnp.where(jnp.broadcast_to(p, (n, BS)) == lane, 1, 0) for p in pick]
     total = (hot[0] + hot[1]) + (hot[2] + hot[3])
     upto = total
@@ -103,8 +105,8 @@
 
 
 def kernel(pat_hbm, tiles_hbm, omega_hbm, gown, skt,
-           tiles, om, csend, crecv, own, ysend, yown, yrecv, zsend, zown, zrecv, probe_t, prefix, sk, skown,
-           xrecv, zsum, zpiece, skrecv, gpart, grecv, gsum, gzrecv, pat, meta, order, ssem, rsem, lsem):
+           tiles, om, csend, crecv, own, ysend, yrecv, zsend, zown, zrecv, probe_t, prefix, sk,
+           xrecv, zpiece, skrecv, gpart, grecv, gsum, gzrecv, pat, meta, order, ssem, rsem, lsem):
     r = lax.axis_index("row")
     c = lax.axis_index("col")
     zl, x = r // 4, r % 4
@@ -117,6 +119,8 @@
     ys = [(y + d) % 4 for d in range(4)]
     zs = [(zh * 4 + zl + d) % 8 for d in range(8)]
 
+    nearest = [jnp.where(zl == 0, a, jnp.where(zl == 3, b, e)) for a, b, e in ((3, 1, 1), (2, 2, 3), (1, 3, 2))]
+
     def plane(d):
         return dev(x=xs[d // 4], y=ys[d % 4])
 
@@ -132,11 +136,32 @@
 
     def sent(ref, sem):
         pltpu.make_async_copy(ref, ref, ssem.at[sem]).wait()
+
+    def drain(parts):
+        for n in range(3):
+            sent(zpiece.at[n], OM_Z + n)
+            if parts == 3:
+                sent(zpiece.at[n], SK_Z + n)
+        for n in range(4):
+            for j in range(3):
+                sent(zsend.at[n], OM_X + n * 4 + j)
+                if parts > 1:
+                    sent(zsend.at[n], Y_G + n * 4 + j)
+            if parts > 1:
+                sent(csend.at[n], CORE_R + n)
+                sent(csend.at[n], CORE_G + n)
+                sent(zsend.at[n], Z_R + n)
+            for j in range(6):
+                if parts > 1 and j % 2 == 0:
+                    sent(zsend.at[n], Y_R + n * 6 + j)
+                if parts == 3:
+                    sent(sk.at[n, j], SK_X + n * 6 + j)
 
     load_pattern = pltpu.make_async_copy(pat_hbm, pat, lsem.at[2])
     load_pattern.start()
     load_tiles = pltpu.make_async_copy(tiles_hbm, tiles.at[pl.ds(0, 64)], lsem.at[0])
     load_tiles.start()
+    load_order = pltpu.make_async_copy(meta, order, lsem.at[3])
     mine = om.at[pl.ds(2 * r, 2)]
     load_omega = pltpu.make_async_copy(omega_hbm, mine, lsem.at[1])
     load_omega.start()
@@ -147,36 +172,38 @@
         for d in range(1, 16):
             pl.semaphore_signal(barrier, inc=1, device_id=plane(d), device_id_type=MESH)
             pl.semaphore_signal(barrier, inc=1, device_id=column(d), device_id_type=MESH)
-        load_omega.wait()
-        pl.semaphore_wait(barrier, 30)
-
-    load_order = pltpu.make_async_copy(meta, order, lsem.at[3])
-
-    with jax.named_scope("omega_gather"):
-        for d in (3, 2, 1):
-            send(mine, mine, OM_Z + d - 1, dev(zl=(zl + d) % 4))
-        for dx in (1, 2, 3):
-            send(mine, mine, OM_X + dx - 1, dev(x=(x + dx) % 4))
         tiles[64, 0] = jnp.zeros((BS, BS), BF16)
         probe_t[64] = jnp.zeros((BS, BS), BF16)
         load_pattern.wait()
         sort_tiles(pat, meta)
         load_order.start()
-        for d in (1, 2, 3):
-            block = om.at[pl.ds(2 * (((zl + 4 - d) % 4) * 4 + x), 2)]
-            got(block, OM_Z + d - 1)
-            for dx in (1, 2, 3):
-                send(block, block, OM_X + d * 3 + dx - 1, dev(x=(x + dx) % 4))
+        load_omega.wait()
+        pl.semaphore_wait(barrier, 30)
+
+    with jax.named_scope("omega_gather"):
+        for d in nearest:
+            send(mine, mine, OM_Z + 3 - d, dev(zl=(zl + 4 - d) % 4))
+
+        def rows_of(back, dx):
+            return 2 * (((zl + 4 - back) % 4) * 4 + xs[dx])
+
+        def pass_on(n, back):
+            block = om.at[pl.ds(rows_of(back, 0), 2)]
+            if n:
+                got(block, OM_Z + back - 1)
+            send(block, block, OM_X + n * 4, dev(x=xs[1]))
+            send(block, block, OM_X + n * 4 + 1, dev(x=xs[3]))
+            send(block, block, OM_X + n * 4 + 2, dev(x=xs[2]))
+
+        pass_on(0, 0)
+        pass_on(1, nearest[0])
+        pass_on(2, nearest[1])
+        pass_on(3, nearest[2])
         load_tiles.wait()
         load_order.wait()
-        for d in range(4):
-            for dx in (1, 2, 3):
-                got(om.at[pl.ds(2 * (((zl + 4 - d) % 4) * 4 + (x + 4 - dx) % 4), 2)], OM_X + d * 3 + dx - 1)
-        for d in (1, 2, 3):
-            sent(mine, OM_Z + d - 1)
-        for d in range(4):
-            for dx in (1, 2, 3):
-                sent(mine, OM_X + d * 3 + dx - 1)
+        for n, back in enumerate([0] + nearest):
+            for j, dx in ((0, 3), (1, 1), (2, 2)):
+                got(om.at[pl.ds(rows_of(back, dx), 2)], OM_X + n * 4 + j)
 
     def product(i):
         left = jnp.concatenate([tiles[i, t] for t in range(4)], axis=1)
@@ -196,24 +223,25 @@
         send(csend.at[m], crecv.at[m], CORE_R + m, dev(k=1 - k))
         lax.fori_loop(0, 8, for_own, 0, unroll=True)
 
+    def partial(m, dy, b):
+        at = ys[dy] * 2 + b
+        return own[m, at] + crecv[m, at].astype(F32)
+
     def along_y(m):
         got(crecv.at[m], CORE_R + m)
-        for d in (1, 2, 3, 0):
-            b = ((y + d) % 4) * 2
-            total = own[m, pl.ds(b, 2)] + crecv[m, pl.ds(b, 2)].astype(F32)
-            if d:
-                ysend[m, d - 1] = total.astype(BF16)
-                send(ysend.at[m, d - 1], yrecv.at[m, d - 1], Y_R + m * 3 + d - 1, dev(y=(y + d) % 4))
-            else:
-                yown[m] = total
+        for j, dy in ((0, 1), (2, 2), (4, 3)):
+            for b in range(2):
+                ysend[m, j + b] = partial(m, dy, b).astype(BF16)
+            send(ysend.at[m, pl.ds(j, 2)], yrecv.at[m, pl.ds(j, 2)], Y_R + m * 6 + j, dev(y=ys[dy]))
 
     def across_z(m):
-        total = yown[m]
-        for d in (1, 2, 3):
-            got(yrecv.at[m, d - 1], Y_R + m * 3 + d - 1)
-            total += yrecv[m, d - 1].astype(F32)
-        zown[m] = total
-        zsend[m] = total.astype(BF16)
+        for j in (0, 2, 4):
+            got(yrecv.at[m, pl.ds(j, 2)], Y_R + m * 6 + j)
+        for b in range(2):
+            total = (partial(m, 0, b) + yrecv[m, b].astype(F32)) + (
+                yrecv[m, 2 + b].astype(F32) + yrecv[m, 4 + b].astype(F32))
+            zown[m, b] = total
+            zsend[m, b] = total.astype(BF16)
         send(zsend.at[m], zrecv.at[m], Z_R + m, dev(zh=1 - zh))
 
     def gather_y(m):
@@ -223,45 +251,24 @@
         for b in range(2):
             probe_t[at + b] = total[b].T.astype(BF16)
         part = probe_t.at[pl.ds(at, 2)]
-        for d in (1, 2, 3):
-            send(part, part, Y_G + m * 3 + d - 1, dev(y=(y + d) % 4))
+        send(part, part, Y_G + m * 4, dev(y=ys[1]))
+        send(part, part, Y_G + m * 4 + 1, dev(y=ys[3]))
+        send(part, part, Y_G + m * 4 + 2, dev(y=ys[2]))
 
     def gather_core(m):
-        for d in (1, 2, 3):
-            got(probe_t.at[pl.ds((k * 4 + m) * 8 + ((y + 4 - d) % 4) * 2, 2)], Y_G + m * 3 + d - 1)
+        for j, dy in ((0, 3), (1, 1), (2, 2)):
+            got(probe_t.at[pl.ds((k * 4 + m) * 8 + ys[dy] * 2, 2)], Y_G + m * 4 + j)
         part = probe_t.at[pl.ds((k * 4 + m) * 8, 8)]
         send(part, part, CORE_G + m, dev(k=1 - k))
 
     with jax.named_scope("probe_sum"):
-        value_part(0)
-        along_y(0)
-        value_part(1)
-        along_y(1)
-        value_part(2)
-        along_y(2)
-        across_z(0)
-        value_part(3)
-        along_y(3)
-        across_z(1)
-        across_z(2)
-        gather_y(0)
-        across_z(3)
-        gather_y(1)
-        gather_y(2)
-        gather_core(0)
-        gather_y(3)
-        gather_core(1)
-        gather_core(2)
-        gather_core(3)
+        for step, m in ((value_part, 0), (along_y, 0), (value_part, 1), (along_y, 1), (value_part, 2), (along_y, 2),
+                        (across_z, 0), (value_part, 3), (along_y, 3), (across_z, 1), (across_z, 2), (gather_y, 0),
+                        (across_z, 3), (gather_y, 1), (gather_y, 2), (gather_core, 0), (gather_y, 3), (gather_core, 1),
+                        (gather_core, 2), (gather_core, 3)):
+            step(m)
         for m in range(4):
             got(probe_t.at[pl.ds(((1 - k) * 4 + m) * 8, 8)], CORE_G + m)
-        for m in range(4):
-            sent(csend.at[m], CORE_R + m)
-            sent(zsend.at[m], Z_R + m)
-            sent(crecv.at[m], CORE_G + m)
-            for d in range(3):
-                sent(ysend.at[m, d], Y_R + m * 3 + d)
-                sent(ysend.at[m, d], Y_G + m * 3 + d)
 
     with jax.named_scope("sketch_value"):
         def term(q, acc):
@@ -278,36 +285,47 @@
         def block_sum(p):
             return prefix[order[2, p]] * order[3, p].astype(F32)
 
-        for dz in (1, 2, 3, 0):
-            for dx in (1, 2, 3):
-                to = ((zl + dz) % 4) * 4 + (x + dx) % 4
-                for b in range(2):
-                    sk[dz, dx - 1, b] = block_sum(2 * to + b).astype(BF16)
-                send(sk.at[dz, dx - 1], xrecv.at[dz, dx - 1], SK_X + dz * 3 + dx - 1, dev(x=(x + dx) % 4))
-        for dz in (1, 2, 3, 0):
+        order_z = nearest[::-1] + [0]
+
+        def term_of(n, dx, b):
+            return block_sum(2 * (((zl + 4 - order_z[n]) % 4) * 4 + xs[dx]) + b)
+
+        def send_x(n, j, value):
+            sk[n, j] = value.astype(BF16)
+            send(sk.at[n, j], xrecv.at[n, j], SK_X + n * 6 + j, dev(x=xs[1 if j % 2 == 0 else 3]))
+
+        def got_x(n, j):
+            got(xrecv.at[n, j], SK_X + n * 6 + j)
+            return xrecv[n, j].astype(F32)
+
+        def along_x(n):
+            send_x(n, 0, term_of(n, 2, 0))
+            send_x(n, 1, term_of(n, 2, 1))
+            send_x(n, 2, term_of(n, 1, 1))
+            send_x(n, 3, term_of(n, 3, 0))
+
+        def relay_x(n):
+            send_x(n, 4, term_of(n, 1, 0) + got_x(n, 0))
+            send_x(n, 5, term_of(n, 3, 1) + got_x(n, 1))
+
+        def across_zl(n):
+            total = [term_of(n, 0, b) + got_x(n, i) + got_x(n, j) for b, (i, j) in enumerate(((3, 4), (2, 5)))]
+            if n == 3:
+                return total
             for b in range(2):
-                skown[dz, b] = block_sum(2 * (((zl + dz) % 4) * 4 + x) + b)
-        for dz in (1, 2, 3, 0):
-            total = skown[dz]
-            for dx in (1, 2, 3):
-                got(xrecv.at[dz, dx - 1], SK_X + dz * 3 + dx - 1)
-                total += xrecv[dz, dx - 1].astype(F32)
-            if dz:
-                zpiece[dz - 1] = total.astype(BF16)
-                send(zpiece.at[dz - 1], skrecv.at[dz - 1], SK_Z + dz - 1, dev(zl=(zl + dz) % 4))
-            else:
-                zsum[...] = total
-        total = zsum[...]
-        for dz in (1, 2, 3):
-            got(skrecv.at[dz - 1], SK_Z + dz - 1)
-            total += skrecv[dz - 1].astype(F32)
-        skt[:, :BS] = total[0]
-        skt[:, BS:] = total[1]
-        for dz in range(4):
-            for dx in range(3):
-                sent(sk.at[dz, dx], SK_X + dz * 3 + dx)
-        for dz in range(3):
-            sent(zpiece.at[dz], SK_Z + dz)
+                zpiece[n, b] = total[b].astype(BF16)
+            send(zpiece.at[n], skrecv.at[3 - order_z[n]], SK_Z + 3 - order_z[n], dev(zl=(zl + 4 - order_z[n]) % 4))
+
+        for step, n in ((along_x, 0), (along_x, 1), (relay_x, 0), (along_x, 2), (relay_x, 1), (along_x, 3), (relay_x, 2),
+                        (across_zl, 0), (relay_x, 3), (across_zl, 1), (across_zl, 2)):
+            step(n)
+        total = across_zl(3)
+        for d in range(3):
+            got(skrecv.at[d], SK_Z + d)
+            for b in range(2):
+                total[b] += skrecv[d, b].astype(F32)
+        for b in range(2):
+            skt[:, b * BS:(b + 1) * BS] = total[b]
 
     with jax.named_scope("gram_sum"):
         g = lax.dot_general(skt[...], skt[...], (((1,), (1,)), ((), ())), precision=lax.Precision.HIGHEST,
@@ -339,6 +357,7 @@
             sent(gsum, GR_P + d)
             sent(gsum, GR_Z + d)
             sent(gsum, GR_G + d)
+        drain(3)
 
 
 def finish(scale, gram, skt, out_ref, work):
@@ -362,25 +381,22 @@
             vmem((4, 8, BS, BS), BF16),
             vmem((4, 8, BS, BS), BF16),
             vmem((4, 8, BS, BS), F32),
-            vmem((4, 3, 2, BS, BS), BF16),
-            vmem((4, 2, BS, BS), F32),
-            vmem((4, 3, 2, BS, BS), BF16),
+            vmem((4, 6, BS, BS), BF16),
+            vmem((4, 6, BS, BS), BF16),
             vmem((4, 2, BS, BS), BF16),
             vmem((4, 2, BS, BS), F32),
             vmem((4, 2, BS, BS), BF16),
             vmem((65, BS, BS), BF16),
             vmem((PAIRS, BS, BS), F32),
-            vmem((4, 3, 2, BS, BS), BF16),
-            vmem((4, 2, BS, BS), F32),
-            vmem((4, 3, 2, BS, BS), BF16),
-            vmem((2, BS, BS), F32),
+            vmem((4, 6, BS, BS), BF16),
+            vmem((4, 6, BS, BS), BF16),
             vmem((3, 2, BS, BS), BF16),
             vmem((3, 2, BS, BS), BF16),
             vmem((16, 8, BS), F32),
             vmem((15, 8, BS), F32),
             vmem((8, BS), F32),
             vmem((15, 8, BS), F32),
-            vmem((64, 4), jnp.int32),
+            vmem((4, 64), jnp.int32),
             vmem((8, 3 * BS), jnp.int32),
             pltpu.SMEM((8, 3 * BS), jnp.int32),
             pltpu.SemaphoreType.DMA((N_SEM,)),
@@ -390,7 +406,7 @@
         compiler_params=pltpu.CompilerParams(
             collective_id=0, has_side_effects=True, vmem_limit_bytes=56 * 1024 * 1024),
         cost_estimate=pl.CostEstimate(flops=2 * 2 * 256 * BS ** 3, bytes_accessed=9 * 2 ** 20, transcendentals=0),
-    )(pattern, tiles, omega.reshape(2, BS, BS))
+    )(pattern.T, tiles, omega.reshape(2, BS, BS))
     return pl.pallas_call(
         functools.partial(finish, scale),
         name="cholesky_basis",

time: 103 us -> 98.5 us (0.956)
  Pallas kernels: 101 us -> 98.4 us
  local copies, waits for them, and re-layouts: 1.38 us -> 0 us
    pallas_call x1, Pallas kernels: 95.1 us -> 92.1 us  [local(): pl.pallas_call(kernel, name='gauss_newton_sketch', out_shape=[jax.ShapeDt...]
    unnamed x1 -> x0, local copies, waits for them, and re-layouts: 1.38 us -> none
where the time goes in v3:
time: 98.5 us; the launch traced here: 98.4 us
  Pallas kernels  98.4 us (100%)
    pallas_call x1, Pallas kernels, local(): pl.pallas_call(kernel, name='gauss_newton_sketch', out_shape=[jax.ShapeDt...  92.1 us
    pallas_call x1, Pallas kernels, local(): pl.pallas_call(functools.partial(finish, scale), name='cholesky_basis', o...  6.35 us

profile of v3, /device:TPU:1, one launch (start us, length us, event | category | flops | bytes accessed | tf_op | source)
XLA Modules:
  0.0 98.4 jit_solution(3014919773036447607)
XLA Ops:
  0.0 92.1 %gauss_newton_sketch.1 = (f32[16,8,128]{2,1,0:T(8,128)}, f32[128,256]{1,0:T(8,128)}) custom-call(s32[4,64]{1,0:T(4,128)} %bitcast.3, bf16[64,4,128,128]{3,2,1,0:T(8,128)(2,1)} %tiles_hbm.1, bf16[2,128,128]{2,1,0:T(8,128)(2,1)} %bitcast.2), custom_call_target="tpu_custom_call" | custom-call | flops 2147483648 | bytes 9437184 | tf_op jit(solution)/shard_map/gauss_newton_sketch/pallas_call | solution.py:372
  92.1 6.3 %cholesky_basis.1 = f32[256,128]{1,0:T(8,128)} custom-call(f32[16,8,128]{2,1,0:T(8,128)} %get-tuple-element.7.gram, f32[128,256]{1,0:T(8,128)} %get-tuple-element.8.skt), custom_call_target="tpu_custom_call" | custom-call | tf_op jit(solution)/shard_map/cholesky_basis/pallas_call | solution.py:410

commit v4 on v3

--- a/solution.py
+++ b/solution.py
@@ -13,8 +13,8 @@
 BF16 = jnp.bfloat16
 
 OM_Z, OM_X, CORE_R, Y_R, Z_R, Y_G, CORE_G, SK_X, SK_Z, GR_P, GR_Z, GR_G = (
-    0, 3, 19, 23, 47, 51, 67, 71, 95, 98, 114, 130)
-N_SEM = 146
+    0, 3, 19, 23, 47, 55, 79, 83, 107, 110, 126, 142)
+N_SEM = 158
 PAIRS = 144
 
 
@@ -145,15 +145,15 @@
         for n in range(4):
             for j in range(3):
                 sent(zsend.at[n], OM_X + n * 4 + j)
-                if parts > 1:
-                    sent(zsend.at[n], Y_G + n * 4 + j)
             if parts > 1:
                 sent(csend.at[n], CORE_R + n)
                 sent(csend.at[n], CORE_G + n)
-                sent(zsend.at[n], Z_R + n)
+                sent(zsend.at[n, 0], Z_R + n * 2)
+                sent(zsend.at[n, 0], Z_R + n * 2 + 1)
             for j in range(6):
-                if parts > 1 and j % 2 == 0:
-                    sent(zsend.at[n], Y_R + n * 6 + j)
+                if parts > 1:
+                    sent(zsend.at[n, 0], Y_R + n * 6 + j)
+                    sent(zsend.at[n, 0], Y_G + n * 6 + j)
                 if parts == 3:
                     sent(sk.at[n, j], SK_X + n * 6 + j)
 
@@ -229,44 +229,44 @@
 
     def along_y(m):
         got(crecv.at[m], CORE_R + m)
-        for j, dy in ((0, 1), (2, 2), (4, 3)):
-            for b in range(2):
+        for b in range(2):
+            for j, dy in ((2, 2), (0, 1), (4, 3)):
                 ysend[m, j + b] = partial(m, dy, b).astype(BF16)
-            send(ysend.at[m, pl.ds(j, 2)], yrecv.at[m, pl.ds(j, 2)], Y_R + m * 6 + j, dev(y=ys[dy]))
-
-    def across_z(m):
+                send(ysend.at[m, j + b], yrecv.at[m, j + b], Y_R + m * 6 + j + b, dev(y=ys[dy]))
+
+    def across_z(m, b):
         for j in (0, 2, 4):
-            got(yrecv.at[m, pl.ds(j, 2)], Y_R + m * 6 + j)
+            got(yrecv.at[m, j + b], Y_R + m * 6 + j + b)
+        total = (partial(m, 0, b) + yrecv[m, b].astype(F32)) + (
+            yrecv[m, 2 + b].astype(F32) + yrecv[m, 4 + b].astype(F32))
+        zown[m, b] = total
+        zsend[m, b] = total.astype(BF16)
+        send(zsend.at[m, b], zrecv.at[m, b], Z_R + m * 2 + b, dev(zh=1 - zh))
+
+    def gather_y(m, b):
+        got(zrecv.at[m, b], Z_R + m * 2 + b)
+        at = (k * 4 + m) * 8 + y * 2 + b
+        probe_t[at] = (zown[m, b] + zrecv[m, b].astype(F32)).T.astype(BF16)
+        part = probe_t.at[at]
+        for j, dy in ((2, 2), (0, 1), (4, 3)):
+            send(part, part, Y_G + m * 6 + j + b, dev(y=ys[dy]))
+
+    def gather_core(m):
         for b in range(2):
-            total = (partial(m, 0, b) + yrecv[m, b].astype(F32)) + (
-                yrecv[m, 2 + b].astype(F32) + yrecv[m, 4 + b].astype(F32))
-            zown[m, b] = total
-            zsend[m, b] = total.astype(BF16)
-        send(zsend.at[m], zrecv.at[m], Z_R + m, dev(zh=1 - zh))
-
-    def gather_y(m):
-        got(zrecv.at[m], Z_R + m)
-        total = zown[m] + zrecv[m].astype(F32)
-        at = (k * 4 + m) * 8 + y * 2
-        for b in range(2):
-            probe_t[at + b] = total[b].T.astype(BF16)
-        part = probe_t.at[pl.ds(at, 2)]
-        send(part, part, Y_G + m * 4, dev(y=ys[1]))
-        send(part, part, Y_G + m * 4 + 1, dev(y=ys[3]))
-        send(part, part, Y_G + m * 4 + 2, dev(y=ys[2]))
-
-    def gather_core(m):
-        for j, dy in ((0, 3), (1, 1), (2, 2)):
-            got(probe_t.at[pl.ds((k * 4 + m) * 8 + ys[dy] * 2, 2)], Y_G + m * 4 + j)
+            for j, dy in ((2, 2), (0, 3), (4, 1)):
+                got(probe_t.at[(k * 4 + m) * 8 + ys[dy] * 2 + b], Y_G + m * 6 + j + b)
         part = probe_t.at[pl.ds((k * 4 + m) * 8, 8)]
         send(part, part, CORE_G + m, dev(k=1 - k))
 
     with jax.named_scope("probe_sum"):
-        for step, m in ((value_part, 0), (along_y, 0), (value_part, 1), (along_y, 1), (value_part, 2), (along_y, 2),
-                        (across_z, 0), (value_part, 3), (along_y, 3), (across_z, 1), (across_z, 2), (gather_y, 0),
-                        (across_z, 3), (gather_y, 1), (gather_y, 2), (gather_core, 0), (gather_y, 3), (gather_core, 1),
-                        (gather_core, 2), (gather_core, 3)):
-            step(m)
+        for step, *part in (
+                (value_part, 0), (along_y, 0), (value_part, 1), (along_y, 1), (value_part, 2), (along_y, 2),
+                (across_z, 0, 0), (across_z, 0, 1), (value_part, 3), (along_y, 3), (across_z, 1, 0), (across_z, 1, 1),
+                (across_z, 2, 0), (gather_y, 0, 0), (across_z, 2, 1), (gather_y, 0, 1), (across_z, 3, 0),
+                (gather_y, 1, 0), (across_z, 3, 1), (gather_y, 1, 1), (gather_y, 2, 0), (gather_core, 0),
+                (gather_y, 2, 1), (gather_y, 3, 0), (gather_core, 1), (gather_y, 3, 1), (gather_core, 2),
+                (gather_core, 3)):
+            step(*part)
         for m in range(4):
             got(probe_t.at[pl.ds(((1 - k) * 4 + m) * 8, 8)], CORE_G + m)
 

time: 98.5 us -> 97.4 us (0.989)
  Pallas kernels: 98.4 us -> 97.3 us
    pallas_call x1, Pallas kernels: 92.1 us -> 90.9 us  [local(): pl.pallas_call(kernel, name='gauss_newton_sketch', out_shape=[jax.ShapeDt...]
where the time goes in v4:
time: 97.4 us; the launch traced here: 97.3 us
  Pallas kernels  97.3 us (100%)
    pallas_call x1, Pallas kernels, local(): pl.pallas_call(kernel, name='gauss_newton_sketch', out_shape=[jax.ShapeDt...  90.9 us
    pallas_call x1, Pallas kernels, local(): pl.pallas_call(functools.partial(finish, scale), name='cholesky_basis', o...  6.35 us

profile of v4, /device:TPU:1, one launch (start us, length us, event | category | flops | bytes accessed | tf_op | source)
XLA Modules:
  0.0 97.3 jit_solution(16537986150776397514)
XLA Ops:
  0.0 90.9 %gauss_newton_sketch.1 = (f32[16,8,128]{2,1,0:T(8,128)}, f32[128,256]{1,0:T(8,128)}) custom-call(s32[4,64]{1,0:T(4,128)} %bitcast.3, bf16[64,4,128,128]{3,2,1,0:T(8,128)(2,1)} %tiles_hbm.1, bf16[2,128,128]{2,1,0:T(8,128)(2,1)} %bitcast.2), custom_call_target="tpu_custom_call" | custom-call | flops 2147483648 | bytes 9437184 | tf_op jit(solution)/shard_map/gauss_newton_sketch/pallas_call | solution.py:372
  90.9 6.3 %cholesky_basis.1 = f32[256,128]{1,0:T(8,128)} custom-call(f32[16,8,128]{2,1,0:T(8,128)} %get-tuple-element.7.gram, f32[128,256]{1,0:T(8,128)} %get-tuple-element.8.skt), custom_call_target="tpu_custom_call" | custom-call | tf_op jit(solution)/shard_map/cholesky_basis/pallas_call | solution.py:410

commit v5 on v4

--- a/solution.py
+++ b/solution.py
@@ -13,8 +13,8 @@
 BF16 = jnp.bfloat16
 
 OM_Z, OM_X, CORE_R, Y_R, Z_R, Y_G, CORE_G, SK_X, SK_Z, GR_P, GR_Z, GR_G = (
-    0, 3, 19, 23, 47, 55, 79, 83, 107, 110, 126, 142)
-N_SEM = 158
+    0, 6, 30, 34, 58, 66, 90, 94, 118, 124, 140, 156)
+N_SEM = 172
 PAIRS = 144
 
 
@@ -139,12 +139,13 @@
 
     def drain(parts):
         for n in range(3):
-            sent(zpiece.at[n], OM_Z + n)
-            if parts == 3:
-                sent(zpiece.at[n], SK_Z + n)
+            for b in range(2):
+                sent(zpiece.at[n, b], OM_Z + n * 2 + b)
+                if parts == 3:
+                    sent(zpiece.at[n, b], SK_Z + n * 2 + b)
         for n in range(4):
-            for j in range(3):
-                sent(zsend.at[n], OM_X + n * 4 + j)
+            for j in range(6):
+                sent(zsend.at[n, 0], OM_X + n * 6 + j)
             if parts > 1:
                 sent(csend.at[n], CORE_R + n)
                 sent(csend.at[n], CORE_G + n)
@@ -182,18 +183,20 @@
 
     with jax.named_scope("omega_gather"):
         for d in nearest:
-            send(mine, mine, OM_Z + 3 - d, dev(zl=(zl + 4 - d) % 4))
+            for b in range(2):
+                block = om.at[2 * r + b]
+                send(block, block, OM_Z + (3 - d) * 2 + b, dev(zl=(zl + 4 - d) % 4))
 
         def rows_of(back, dx):
             return 2 * (((zl + 4 - back) % 4) * 4 + xs[dx])
 
         def pass_on(n, back):
-            block = om.at[pl.ds(rows_of(back, 0), 2)]
-            if n:
-                got(block, OM_Z + back - 1)
-            send(block, block, OM_X + n * 4, dev(x=xs[1]))
-            send(block, block, OM_X + n * 4 + 1, dev(x=xs[3]))
-            send(block, block, OM_X + n * 4 + 2, dev(x=xs[2]))
+            for b in range(2):
+                block = om.at[rows_of(back, 0) + b]
+                if n:
+                    got(block, OM_Z + (back - 1) * 2 + b)
+                for j, dx in ((2, 2), (0, 1), (4, 3)):
+                    send(block, block, OM_X + n * 6 + j + b, dev(x=xs[dx]))
 
         pass_on(0, 0)
         pass_on(1, nearest[0])
@@ -202,8 +205,9 @@
         load_tiles.wait()
         load_order.wait()
         for n, back in enumerate([0] + nearest):
-            for j, dx in ((0, 3), (1, 1), (2, 2)):
-                got(om.at[pl.ds(rows_of(back, dx), 2)], OM_X + n * 4 + j)
+            for j, dx in ((0, 3), (4, 1), (2, 2)):
+                for b in range(2):
+                    got(om.at[rows_of(back, dx) + b], OM_X + n * 6 + j + b)
 
     def product(i):
         left = jnp.concatenate([tiles[i, t] for t in range(4)], axis=1)
@@ -309,20 +313,22 @@
             send_x(n, 5, term_of(n, 3, 1) + got_x(n, 1))
 
         def across_zl(n):
-            total = [term_of(n, 0, b) + got_x(n, i) + got_x(n, j) for b, (i, j) in enumerate(((3, 4), (2, 5)))]
-            if n == 3:
-                return total
-            for b in range(2):
-                zpiece[n, b] = total[b].astype(BF16)
-            send(zpiece.at[n], skrecv.at[3 - order_z[n]], SK_Z + 3 - order_z[n], dev(zl=(zl + 4 - order_z[n]) % 4))
+            total = []
+            for b, (i, j) in enumerate(((3, 4), (2, 5))):
+                total.append(term_of(n, 0, b) + got_x(n, i) + got_x(n, j))
+                if n < 3:
+                    zpiece[n, b] = total[b].astype(BF16)
+                    to = 3 - order_z[n]
+                    send(zpiece.at[n, b], skrecv.at[to, b], SK_Z + to * 2 + b, dev(zl=(zl + 4 - order_z[n]) % 4))
+            return total
 
         for step, n in ((along_x, 0), (along_x, 1), (relay_x, 0), (along_x, 2), (relay_x, 1), (along_x, 3), (relay_x, 2),
                         (across_zl, 0), (relay_x, 3), (across_zl, 1), (across_zl, 2)):
             step(n)
         total = across_zl(3)
         for d in range(3):
-            got(skrecv.at[d], SK_Z + d)
             for b in range(2):
+                got(skrecv.at[d, b], SK_Z + d * 2 + b)
                 total[b] += skrecv[d, b].astype(F32)
         for b in range(2):
             skt[:, b * BS:(b + 1) * BS] = total[b]

time: 97.4 us -> 96.6 us (level)
  no operation moved by 1% of the time
where the time goes in v5:
time: 96.6 us; the launch traced here: 96.5 us
  Pallas kernels  96.5 us (100%)
    pallas_call x1, Pallas kernels, local(): pl.pallas_call(kernel, name='gauss_newton_sketch', out_shape=[jax.ShapeDt...  90.2 us
    pallas_call x1, Pallas kernels, local(): pl.pallas_call(functools.partial(finish, scale), name='cholesky_basis', o...  6.35 us

profile of v5, /device:TPU:1, one launch (start us, length us, event | category | flops | bytes accessed | tf_op | source)
XLA Modules:
  0.0 96.5 jit_solution(2311456067599885278)
XLA Ops:
  0.0 90.2 %gauss_newton_sketch.1 = (f32[16,8,128]{2,1,0:T(8,128)}, f32[128,256]{1,0:T(8,128)}) custom-call(s32[4,64]{1,0:T(4,128)} %bitcast.3, bf16[64,4,128,128]{3,2,1,0:T(8,128)(2,1)} %tiles_hbm.1, bf16[2,128,128]{2,1,0:T(8,128)(2,1)} %bitcast.2), custom_call_target="tpu_custom_call" | custom-call | flops 2147483648 | bytes 9437184 | tf_op jit(solution)/shard_map/gauss_newton_sketch/pallas_call | solution.py:378
  90.2 6.3 %cholesky_basis.1 = f32[256,128]{1,0:T(8,128)} custom-call(f32[16,8,128]{2,1,0:T(8,128)} %get-tuple-element.7.gram, f32[128,256]{1,0:T(8,128)} %get-tuple-element.8.skt), custom_call_target="tpu_custom_call" | custom-call | tf_op jit(solution)/shard_map/cholesky_basis/pallas_call | solution.py:416

commit v6 on v5

--- a/solution.py
+++ b/solution.py
@@ -161,11 +161,11 @@
     load_pattern = pltpu.make_async_copy(pat_hbm, pat, lsem.at[2])
     load_pattern.start()
     load_tiles = pltpu.make_async_copy(tiles_hbm, tiles.at[pl.ds(0, 64)], lsem.at[0])
-    load_tiles.start()
     load_order = pltpu.make_async_copy(meta, order, lsem.at[3])
     mine = om.at[pl.ds(2 * r, 2)]
     load_omega = pltpu.make_async_copy(omega_hbm, mine, lsem.at[1])
     load_omega.start()
+    load_tiles.start()
 
     with jax.named_scope("barrier"):
         barrier = pltpu.get_barrier_semaphore()
@@ -173,11 +173,6 @@
         for d in range(1, 16):
             pl.semaphore_signal(barrier, inc=1, device_id=plane(d), device_id_type=MESH)
             pl.semaphore_signal(barrier, inc=1, device_id=column(d), device_id_type=MESH)
-        tiles[64, 0] = jnp.zeros((BS, BS), BF16)
-        probe_t[64] = jnp.zeros((BS, BS), BF16)
-        load_pattern.wait()
-        sort_tiles(pat, meta)
-        load_order.start()
         load_omega.wait()
         pl.semaphore_wait(barrier, 30)
 
@@ -199,6 +194,11 @@
                     send(block, block, OM_X + n * 6 + j + b, dev(x=xs[dx]))
 
         pass_on(0, 0)
+        tiles[64, 0] = jnp.zeros((BS, BS), BF16)
+        probe_t[64] = jnp.zeros((BS, BS), BF16)
+        load_pattern.wait()
+        sort_tiles(pat, meta)
+        load_order.start()
         pass_on(1, nearest[0])
         pass_on(2, nearest[1])
         pass_on(3, nearest[2])

time: 96.6 us -> 96.2 us (level)
  no operation moved by 1% of the time
where the time goes in v6:
time: 96.2 us; the launch traced here: 96.1 us
  Pallas kernels  96.1 us (100%)
    pallas_call x1, Pallas kernels, local(): pl.pallas_call(kernel, name='gauss_newton_sketch', out_shape=[jax.ShapeDt...  89.7 us
    pallas_call x1, Pallas kernels, local(): pl.pallas_call(functools.partial(finish, scale), name='cholesky_basis', o...  6.35 us

profile of v6, /device:TPU:1, one launch (start us, length us, event | category | flops | bytes accessed | tf_op | source)
XLA Modules:
  0.0 96.1 jit_solution(17890686716600114752)
XLA Ops:
  0.0 89.7 %gauss_newton_sketch.1 = (f32[16,8,128]{2,1,0:T(8,128)}, f32[128,256]{1,0:T(8,128)}) custom-call(s32[4,64]{1,0:T(4,128)} %bitcast.3, bf16[64,4,128,128]{3,2,1,0:T(8,128)(2,1)} %tiles_hbm.1, bf16[2,128,128]{2,1,0:T(8,128)(2,1)} %bitcast.2), custom_call_target="tpu_custom_call" | custom-call | flops 2147483648 | bytes 9437184 | tf_op jit(solution)/shard_map/gauss_newton_sketch/pallas_call | solution.py:378
  89.7 6.3 %cholesky_basis.1 = f32[256,128]{1,0:T(8,128)} custom-call(f32[16,8,128]{2,1,0:T(8,128)} %get-tuple-element.7.gram, f32[128,256]{1,0:T(8,128)} %get-tuple-element.8.skt), custom_call_target="tpu_custom_call" | custom-call | tf_op jit(solution)/shard_map/cholesky_basis/pallas_call | solution.py:416
